TPU v7x, 256 devices: a whole 4x4x8 slice. The times are simulated.
256 devices in a mesh: src: 16 (over y, z_hi, core), tgt: 16 (over z_lo, x).
Axes of the slice: x: 4, y: 4, z: 8 (z_hi: 2, z_lo: 4; z = z_hi * 4 + z_lo), core: 2. Of those that a mesh axis runs over, the one named last changes fastest.
Arguments:
- source_points: float32 [64, 65536], P(None, ('src', 'tgt')), may hold values from -1.5 to 1.5
- target_points: float32 [64, 65536], P(None, ('src', 'tgt')), may hold values from -1.5 to 1.5
- source_logw: float32 [65536], P(('src', 'tgt')), may hold values from -2 to 2
- target_logw: float32 [65536], P(('src', 'tgt')), may hold values from -2 to 2
- potential_in: float32 [65536], P(('src', 'tgt')), may hold values from -5 to 61
- pair_list: int32 [256, 128, 2], P(('src', 'tgt')), may hold values from 0 to 255, as said below
- pair_counts: int32 [256], P(('src', 'tgt')), may hold values from 16 to 128, as said below
Outputs:
- source_potential: float32 [65536], P(('src', 'tgt'))
- target_potential: float32 [65536], P(('src', 'tgt'))
Inputs may be any that keep to these rules, and one draw needn't show every extreme that they name: `pair_list`: for row d = s * 16 + t, every source block lies in s * 16 to s * 16 + 15 and every target block equals t modulo 16; the entries of a row are distinct; only the first pair_counts[d] are live, later ones are ignored. Every source block and every target block whose ranges a row covers appears in a live pair of that row. `pair_counts`: some row has exactly 128 live pairs.
All inputs are finite; a program needn't handle non-finite values.
Results may differ from a plain program's by a relative error of at most 0.0003.
Values sent between devices are 32-bit elements; how exact they have to be, the bound alone decides.
No kernel may reach another device: no remote copies, remote signals or barrier semaphores. Data moves between devices by JAX's collectives and lax.ppermute only.
A program may use at most 64 MiB of HBM per device.

v0:
```python
import jax
import jax.numpy as jnp
from jax import lax
from jax.sharding import PartitionSpec as P

epsilon = 0.25
lowest_log = -1e30


def merge_pair(first, second):
    highest = jnp.maximum(first[0], second[0])
    summed = first[1] * jnp.exp(first[0] - highest) + second[1] * jnp.exp(second[0] - highest)
    return (highest, summed)


def cross_cost(left_all, left_sq, row_id, right_all, right_sq, col_id, block_len):
    left_points = lax.dynamic_slice_in_dim(left_all, row_id * block_len, block_len, 1)
    right_points = lax.dynamic_slice_in_dim(right_all, col_id * block_len, block_len, 1)
    left_norm = lax.dynamic_slice_in_dim(left_sq, row_id * block_len, block_len, 0)
    right_norm = lax.dynamic_slice_in_dim(right_sq, col_id * block_len, block_len, 0)
    inner_prod = lax.dot_general(
        left_points,
        right_points,
        (((0,), (0,)), ((), ())),
        precision=lax.Precision.HIGHEST,
        preferred_element_type=jnp.float32,
    )
    return left_norm[:, None] + right_norm[None, :] - 2.0 * inner_prod


def fold_part(running, position, highest, summed):
    old_high = lax.dynamic_slice_in_dim(running[0], position, 1, 0)[0]
    old_sum = lax.dynamic_slice_in_dim(running[1], position, 1, 0)[0]
    new_high, new_sum = merge_pair((old_high, old_sum), (highest, summed))
    return (
        lax.dynamic_update_slice_in_dim(running[0], new_high[None, :], position, 0),
        lax.dynamic_update_slice_in_dim(running[1], new_sum[None, :], position, 0),
    )


def on_device(
    source_points, target_points, source_logw, target_logw, potential_in, pair_list, pair_counts
):
    n_tgt = lax.axis_size("tgt")
    n_src = lax.axis_size("src")
    block_len = source_points.shape[1]
    group_points, group_logw = (
        lax.all_gather(source_points, "tgt", axis=1, tiled=True),
        lax.all_gather(source_logw, "tgt", axis=0, tiled=True),
    )
    column_points, column_g = (
        lax.all_gather(target_points, "src", axis=1, tiled=True),
        lax.all_gather(potential_in, "src", axis=0, tiled=True),
    )
    group_sq = jnp.sum(group_points * group_points, axis=0)
    column_sq = jnp.sum(column_points * column_points, axis=0)
    row_start = (
        jnp.full((n_tgt, block_len), lowest_log, dtype=jnp.float32),
        jnp.zeros((n_tgt, block_len), dtype=jnp.float32),
    )
    col_start = (
        jnp.full((n_src, block_len), lowest_log, dtype=jnp.float32),
        jnp.zeros((n_src, block_len), dtype=jnp.float32),
    )
    own_entries = pair_list[0]
    own_count = pair_counts[0]

    def row_visit_pair(slot_id, carry):
        row_id = own_entries[slot_id, 0] % n_tgt
        col_id = own_entries[slot_id, 1] // n_tgt
        tile_cost = cross_cost(
            group_points, group_sq, row_id, column_points, column_sq, col_id, block_len
        )
        g_piece = lax.dynamic_slice_in_dim(column_g, col_id * block_len, block_len, 0)
        scores = (g_piece[None, :] - tile_cost) / epsilon
        highest = jnp.max(scores, axis=1)
        summed = jnp.sum(jnp.exp(scores - highest[:, None]), axis=1)
        return fold_part(carry, row_id, highest, summed)

    row_parts = lax.fori_loop(0, own_count, row_visit_pair, row_start)
    row_high = lax.pmax(row_parts[0], "tgt")
    row_sum = lax.psum(row_parts[1] * jnp.exp(row_parts[0] - row_high), "tgt")
    f_group = epsilon * group_logw - epsilon * (row_high + jnp.log(row_sum)).reshape(-1)
    f_own = lax.dynamic_slice_in_dim(f_group, lax.axis_index("tgt") * block_len, block_len, 0)

    def col_visit_pair(slot_id, carry):
        row_id = own_entries[slot_id, 0] % n_tgt
        col_id = own_entries[slot_id, 1] // n_tgt
        tile_cost = cross_cost(
            group_points, group_sq, row_id, column_points, column_sq, col_id, block_len
        )
        f_piece = lax.dynamic_slice_in_dim(f_group, row_id * block_len, block_len, 0)
        scores = (f_piece[:, None] - tile_cost) / epsilon
        highest = jnp.max(scores, axis=0)
        summed = jnp.sum(jnp.exp(scores - highest[None, :]), axis=0)
        return fold_part(carry, col_id, highest, summed)

    col_parts = lax.fori_loop(0, own_count, col_visit_pair, col_start)
    col_high = lax.pmax(col_parts[0], "src")
    col_sum = lax.psum(col_parts[1] * jnp.exp(col_parts[0] - col_high), "src")
    own_high = lax.dynamic_slice_in_dim(col_high, lax.axis_index("src"), 1, 0)[0]
    own_sum = lax.dynamic_slice_in_dim(col_sum, lax.axis_index("src"), 1, 0)[0]
    g_own = epsilon * target_logw - epsilon * (own_high + jnp.log(own_sum))
    return (f_own, g_own)


def solution(mesh):
    return jax.shard_map(
        on_device,
        mesh=mesh,
        in_specs=(
            P(None, ("src", "tgt")),
            P(None, ("src", "tgt")),
            P(("src", "tgt")),
            P(("src", "tgt")),
            P(("src", "tgt")),
            P(("src", "tgt"), None, None),
            P(("src", "tgt")),
        ),
        out_specs=(P(("src", "tgt")), P(("src", "tgt"))),
        check_vma=False,
    )
```

profile of v0, /device:TPU:6, one launch (start us, length us, event | category | flops | bytes accessed | tf_op | source)
XLA Modules:
  0.0 2359.3 jit_solution(15304724288737712266)
XLA Ops:
  9.3 33.4 %all-gather.1 = f32[16,1,256]{2,1,0:T(1,128)S(1)} all-gather(f32[1,1,256]{2,1,0:T(1,128)S(1)} %bitcast.43), channel_id=1, replica_groups=mesh['src'=16,'tgt'=16] {'src'}, dimensions={0}, use_global_device_ids=true | all-gather | bytes 17408 | tf_op jit(solution)/shard_map/all_gather | solution.py:53
  43.4 32.8 %all-gather = f32[16,1,256]{2,1,0:T(1,128)S(1)} all-gather(f32[1,1,256]{2,1,0:T(1,128)S(1)} %bitcast.44), channel_id=1, replica_groups=mesh['src'=16,'tgt'=16] {'tgt'}, dimensions={0}, use_global_device_ids=true | all-gather | bytes 17408 | tf_op jit(solution)/shard_map/all_gather | solution.py:49
  76.2 1.3 multiply_reduce_fusion
  77.6 65.8 %all-gather.5.cloned.1.call-done = f32[64,4096]{1,0:T(8,128)} async-done(((f32[64,256]{1,0:T(8,128)}), f32[64,4096]{1,0:T(8,128)}) %all-gather.5.cloned.1.call-update) | async-done | bytes 1048592 | tf_op jit(solution)/shard_map/all_gather | solution.py:48
  143.3 1.3 multiply_reduce_fusion.1
  145.3 413.3 %while.28 = (s32[]{:T(128)}, f32[16,256]{1,0:T(8,128)S(1)}, f32[16,256]{1,0:T(8,128)S(1)}, s32[]{:T(128)}, s32[128,2]{0,1:T(2,128)S(1)}, /*index=5*/f32[4096]{0:...) while((s32[]{:T(128)}, f32[16,256]{1,0:T(8,128)S(1)}, ...), condition=%wide.region_5.6_spmd, body=%wide.region_2.5_spmd.sunk | while | flops 50857000 | bytes 678532 | solution.py:80
  151.2 1.3 fusion.24
  158.5 1.3 fusion.24
  165.9 1.3 fusion.24
  173.3 1.3 fusion.24
  217.5 1.3 fusion.24
  224.9 1.3 fusion.24
  232.2 1.3 fusion.24
  239.6 1.3 fusion.24
  247.0 1.3 fusion.24
  254.3 1.3 fusion.24
  261.7 1.3 fusion.24
  269.1 1.3 fusion.24
  276.4 1.3 fusion.24
  283.8 1.3 fusion.24
  291.2 1.3 fusion.24
  298.5 1.3 fusion.24
  305.9 1.3 fusion.24
  313.3 1.3 fusion.24
  357.5 1.3 fusion.24
  364.9 1.3 fusion.24
  372.2 1.3 fusion.24
  558.6 601.5 %pmax.14 = f32[16,256]{1,0:T(8,128)S(1)} all-reduce(f32[16,256]{1,0:T(8,128)S(1)} %get-tuple-element.266), channel_id=1, replica_groups=mesh['src'=16,'tgt'=16] {'tgt'}, use_global_device_ids=true, to_apply=%region_6.7 | all-reduce | flops 4096 | bytes 32768 | tf_op jit(solution)/shard_map/pmax | solution.py:81
  1160.1 74.2 %psum.14 = f32[16,256]{1,0:T(8,128)S(1)} all-reduce(f32[16,256]{1,0:T(8,128)S(1)} %exponential_multiply_fusion.1), channel_id=1, replica_groups=mesh['src'=16,'tgt'=16] {'tgt'}, use_global_device_ids=true, to_apply=%region_7.8 | all-reduce | flops 4096 | bytes 32768 | tf_op jit(solution)/shard_map/psum | solution.py:82
  1234.4 418.7 %while.29 = (s32[]{:T(128)}, f32[16,256]{1,0:T(8,128)S(1)}, f32[16,256]{1,0:T(8,128)S(1)}, s32[]{:T(128)}, s32[128,2]{0,1:T(2,128)S(1)}, /*index=5*/f32[4096]{0:...) while((s32[]{:T(128)}, f32[16,256]{1,0:T(8,128)S(1)}, ...), condition=%wide.region_11.12_spmd, body=%wide.region_8.11_spmd.sunk | while | flops 50857000 | bytes 678532 | solution.py:98
  1653.1 613.2 %pmax.15 = f32[16,256]{1,0:T(8,128)S(1)} all-reduce(f32[16,256]{1,0:T(8,128)S(1)} %get-tuple-element.268), channel_id=1, replica_groups=mesh['src'=16,'tgt'=16] {'src'}, use_global_device_ids=true, to_apply=%region_12.13 | all-reduce | flops 4096 | bytes 32768 | tf_op jit(solution)/shard_map/pmax | solution.py:99
  2266.4 84.2 %psum.15 = f32[16,256]{1,0:T(8,128)S(1)} all-reduce(f32[16,256]{1,0:T(8,128)S(1)} %exponential_multiply_fusion), channel_id=1, replica_groups=mesh['src'=16,'tgt'=16] {'src'}, use_global_device_ids=true, to_apply=%region_13.14 | all-reduce | flops 4096 | bytes 32768 | tf_op jit(solution)/shard_map/psum | solution.py:100
  (1013 shorter events, 239.8 us)
Async XLA Ops:
  7.2 69.1 %all-gather.7.cloned.1.call-start = ((), (), s32[]{:S(2)}) async-start(), calls=%async_computation.1 | async-start | bytes 1114112 | tf_op jit(solution)/shard_map/all_gather | solution.py:52
  7.9 135.4 %all-gather.5.cloned.1.call-start = ((), (), s32[]{:S(2)}) async-start(), calls=%async_computation | async-start | bytes 1114112 | tf_op jit(solution)/shard_map/all_gather | solution.py:48
  8.7 0.7 copy-start.1
  42.7 0.7 copy-start.2
  144.6 0.7 copy-start
  2351.2 0.7 copy-start.3
Sparse Core Ops, SparseCore 0:
  10.5 58.9 all-gather.6
  71.3 71.9 all-gather.4
where the time goes:
time: 2400 us; the launch traced here: 2360 us
  blocking collectives  1440 us (60%)
  loops' own time  570 us (24%)
  matrix products  147 us (6%)
  local copies, waits for them, and re-layouts  107 us (4%)
  waiting for transfers between devices  67.2 us (3%)
    pmax x1, blocking collectives, on_device(): col_high = lax.pmax(col_parts[0], 'src')  613 us
    pmax x1, blocking collectives, on_device(): row_high = lax.pmax(row_parts[0], 'tgt')  602 us
    another operation x1, loops' own time, on_device(): col_parts = lax.fori_loop(0, own_count, col_visit_pair, col_start)  289 us
    another operation x1, loops' own time, on_device(): row_parts = lax.fori_loop(0, own_count, row_visit_pair, row_start)  281 us
    dot_general x112, matrix products, cross_cost(): lax.dot_general(left_points, right_points, (((0,), (0,)), ((), ())), prec...  147 us
    psum x1, blocking collectives, on_device(): col_sum = lax.psum(col_parts[1] * jnp.exp(col_parts[0] - col_high), 'src')  84.2 us
    psum x1, blocking collectives, on_device(): row_sum = lax.psum(row_parts[1] * jnp.exp(row_parts[0] - row_high), 'tgt')  74.2 us
    all_gather x1, waiting for transfers between devices, on_device(): lax.all_gather(source_points, 'tgt', axis=1, tiled=True)  65.8 us
  transfers between devices with their start and end apart: 2, of which 1 were waited for; matrix products, arithmetic and copies ran while one was open for 0% of the time, Pallas kernels for 0%

commit v1 on v0

--- a/solution.py
+++ b/solution.py
@@ -1,10 +1,22 @@
+import functools
+
 import jax
 import jax.numpy as jnp
 from jax import lax
+from jax.experimental import pallas as pl
+from jax.experimental.pallas import tpu as pltpu
 from jax.sharding import PartitionSpec as P
 
 epsilon = 0.25
 lowest_log = -1e30
+log2e = 1.4426950408889634
+ln2 = 0.6931471805599453
+SIDE = 16
+BLOCK = 256
+FEAT = 64
+ROWS = 72
+UNROLL = 4
+vmem_bytes = 30 * 1024 * 1024
 
 
 def merge_pair(first, second):
@@ -38,20 +50,16 @@
     )
 
 
-def on_device(
+def plain_form(
     source_points, target_points, source_logw, target_logw, potential_in, pair_list, pair_counts
 ):
     n_tgt = lax.axis_size("tgt")
     n_src = lax.axis_size("src")
     block_len = source_points.shape[1]
-    group_points, group_logw = (
-        lax.all_gather(source_points, "tgt", axis=1, tiled=True),
-        lax.all_gather(source_logw, "tgt", axis=0, tiled=True),
-    )
-    column_points, column_g = (
-        lax.all_gather(target_points, "src", axis=1, tiled=True),
-        lax.all_gather(potential_in, "src", axis=0, tiled=True),
-    )
+    group_points = lax.all_gather(source_points, "tgt", axis=1, tiled=True)
+    group_logw = lax.all_gather(source_logw, "tgt", axis=0, tiled=True)
+    column_points = lax.all_gather(target_points, "src", axis=1, tiled=True)
+    column_g = lax.all_gather(potential_in, "src", axis=0, tiled=True)
     group_sq = jnp.sum(group_points * group_points, axis=0)
     column_sq = jnp.sum(column_points * column_points, axis=0)
     row_start = (
@@ -102,6 +110,276 @@
     own_sum = lax.dynamic_slice_in_dim(col_sum, lax.axis_index("src"), 1, 0)[0]
     g_own = epsilon * target_logw - epsilon * (own_high + jnp.log(own_sum))
     return (f_own, g_own)
+
+
+def pack_kernel(x_ref, y_ref, lw_ref, g_ref, xp_ref, yp_ref, xsq_ref, ysq_ref):
+    x = x_ref[...]
+    y = y_ref[...]
+    x_sq = jnp.sum(x * x, axis=0, keepdims=True)
+    y_sq = jnp.sum(y * y, axis=0, keepdims=True)
+    b = (4.0 * log2e) * (g_ref[...] - y_sq)
+    row = lax.broadcasted_iota(jnp.int32, (8, BLOCK), 0)
+    b_max = jnp.max(b, axis=1, keepdims=True)
+    xp_ref[0:FEAT, :] = x
+    xp_ref[FEAT:ROWS, :] = jnp.where(row == 0, lw_ref[...], b_max)
+    yp_ref[0:FEAT, :] = y
+    yp_ref[FEAT:ROWS, :] = jnp.broadcast_to(b, (8, BLOCK))
+    xsq_ref[...] = x_sq
+    ysq_ref[...] = y_sq
+
+
+def pack(x, y, lw, g):
+    return pl.pallas_call(
+        pack_kernel,
+        out_shape=(
+            jax.ShapeDtypeStruct((ROWS, BLOCK), jnp.float32),
+            jax.ShapeDtypeStruct((ROWS, BLOCK), jnp.float32),
+            jax.ShapeDtypeStruct((1, BLOCK), jnp.float32),
+            jax.ShapeDtypeStruct((1, BLOCK), jnp.float32),
+        ),
+        in_specs=[pl.BlockSpec(memory_space=pltpu.VMEM)] * 4,
+        out_specs=[pl.BlockSpec(memory_space=pltpu.VMEM)] * 4,
+        name="pack",
+    )(x, y, lw.reshape(1, BLOCK), g.reshape(1, BLOCK))
+
+
+def row_kernel(
+    count_ref, row_ref, xat_ref, yat_ref, where_ref,
+    x0, x1, x2, x3, y0, y1, y2, y3,
+    s_ref, aux_ref, k_ref,
+    xa, ya, ub, acc, peak,
+):
+    xs = (x0, x1, x2, x3)
+    ys = (y0, y1, y2, y3)
+    b_maxes = [xs[q][p, FEAT + 1 : FEAT + 2, :] for q in range(4) for p in range(4)]
+    shift = functools.reduce(jnp.maximum, b_maxes)
+    x_mean_sq = jnp.zeros((1, 1), jnp.float32)
+    for q in range(4):
+        for p in range(4):
+            at = q * 4 + p
+            x = xs[q][p, 0:FEAT, :]
+            mean = jnp.sum(x, axis=1, keepdims=True) * (1.0 / BLOCK)
+            x_mean_sq = jnp.maximum(x_mean_sq, jnp.sum(mean * mean, axis=0, keepdims=True))
+            x = x * (8.0 * log2e)
+            hi = x.astype(jnp.bfloat16)
+            lo = (x - hi.astype(jnp.float32)).astype(jnp.bfloat16)
+            xa[at, 0:64, :] = hi
+            xa[at, 64:128, :] = lo
+            xa[at, 128:192, :] = hi
+            xa[at, 192:256, :] = lo
+            aux_ref[pl.ds(where_ref[at], 1), :] = xs[q][p, FEAT : FEAT + 1, :]
+    y_sq = jnp.zeros((1, BLOCK), jnp.float32)
+    b_low = jnp.full((1, BLOCK), 1e30, jnp.float32)
+    b_high = jnp.full((1, BLOCK), -1e30, jnp.float32)
+    for q in range(4):
+        for p in range(4):
+            at = q * 4 + p
+            y = ys[q][p, 0:FEAT, :]
+            y_sq = jnp.maximum(y_sq, jnp.sum(y * y, axis=0, keepdims=True))
+            b = ys[q][p, FEAT : FEAT + 1, :] - shift
+            b_low = jnp.minimum(b_low, b)
+            b_high = jnp.maximum(b_high, b)
+            turned = jnp.concatenate([y, y], axis=0).T
+            hi = turned.astype(jnp.bfloat16)
+            lo = (turned - hi.astype(jnp.float32)).astype(jnp.bfloat16)
+            ya[at, :, 0:128] = hi
+            ya[at, :, 128:256] = lo
+            ub[at] = jnp.exp2(jnp.broadcast_to(b, (128, BLOCK)).T)
+    lean = (8.0 * log2e) * jnp.sqrt(x_mean_sq * jnp.max(y_sq, axis=1, keepdims=True))
+    top = jnp.max(b_high, axis=1, keepdims=True)
+    good = (
+        (lean <= 24.0)
+        & (jnp.min(b_low, axis=1, keepdims=True) - top >= -105.0)
+        & (jnp.abs(top) <= 16.0)
+    )
+    aux_ref[16:17, :] = shift
+    aux_ref[17:18, :] = jnp.broadcast_to(top, (1, BLOCK))
+    aux_ref[18:19, :] = shift + top
+    aux_ref[19:24, :] = jnp.zeros((5, BLOCK), jnp.float32)
+
+    acc[...] = jnp.zeros_like(acc)
+    peak[...] = jnp.zeros_like(peak)
+    count = count_ref[0]
+
+    def group(step, carry):
+        for u in range(UNROLL):
+            raw = step * UNROLL + u
+            slot = jnp.minimum(raw, count - 1)
+            xat = xat_ref[slot]
+            yat = yat_ref[slot]
+            scores = jnp.dot(ya[yat], xa[xat], preferred_element_type=jnp.float32)
+            tile = jnp.exp2(scores)
+            short = tile.astype(jnp.bfloat16)
+            k_ref[raw] = short
+            peak[...] = jnp.maximum(peak[...], jnp.max(short.reshape(16, 16, BLOCK), axis=0))
+            weight = ub[yat]
+            left = tile[:, 0:128] * weight
+            right = tile[:, 128:256] * weight
+            live = raw < count
+            row = row_ref[slot]
+            left = jnp.sum(left.reshape(32, 8, 128), axis=0)
+            right = jnp.sum(right.reshape(32, 8, 128), axis=0)
+            acc[row, :, 0:128] += jnp.where(live, left, 0.0)
+            acc[row, :, 128:256] += jnp.where(live, right, 0.0)
+        return carry
+
+    lax.fori_loop(0, pl.cdiv(count, UNROLL), group, 0)
+    total = jnp.sum(acc[...], axis=1)
+    highest = jnp.max(peak[...].astype(jnp.float32), axis=0, keepdims=True)
+    good = good & (jnp.max(highest, axis=1, keepdims=True) <= 1.3e36)
+    s_ref[...] = jnp.where(good, total, jnp.nan)
+
+
+def row_pass(count, row, xat, yat, where, xs, ys):
+    smem = pl.BlockSpec(memory_space=pltpu.SMEM)
+    vmem = pl.BlockSpec(memory_space=pltpu.VMEM)
+    return pl.pallas_call(
+        row_kernel,
+        out_shape=(
+            jax.ShapeDtypeStruct((SIDE, BLOCK), jnp.float32),
+            jax.ShapeDtypeStruct((24, BLOCK), jnp.float32),
+            pltpu.VMEM((128, BLOCK, BLOCK), jnp.bfloat16),
+        ),
+        in_specs=[smem] * 5 + [vmem] * 8,
+        out_specs=[vmem] * 3,
+        scratch_shapes=[
+            pltpu.VMEM((SIDE, BLOCK, BLOCK), jnp.bfloat16),
+            pltpu.VMEM((SIDE, BLOCK, BLOCK), jnp.bfloat16),
+            pltpu.VMEM((SIDE, BLOCK, 128), jnp.float32),
+            pltpu.VMEM((SIDE, 8, BLOCK), jnp.float32),
+            pltpu.VMEM((16, BLOCK), jnp.bfloat16),
+        ],
+        compiler_params=pltpu.CompilerParams(vmem_limit_bytes=vmem_bytes),
+        name="row_pass",
+    )(count, row, xat, yat, where, *xs, *ys)
+
+
+def col_kernel(
+    count_ref, row_ref, col_ref, own_ref, s_ref, aux_ref, sq_ref, k_ref,
+    f_ref, t_ref,
+    vp, acc,
+):
+    own = own_ref[0]
+    total = s_ref[...]
+    logw = aux_ref[0:16, :]
+    v = jnp.exp(logw) / total * jnp.exp2(aux_ref[17:18, :])
+    fine = jnp.where((total >= 1.5e-11) & (total <= 4.3e12), 1.0, 0.0)
+    fine = jnp.min(jnp.min(fine, axis=1, keepdims=True), axis=0, keepdims=True) > 0.5
+    v = jnp.where(fine, v, jnp.nan)
+    hi = v.astype(jnp.bfloat16)
+    rest = v - hi.astype(jnp.float32)
+    mid = rest.astype(jnp.bfloat16)
+    low = (rest - mid.astype(jnp.float32)).astype(jnp.bfloat16)
+    lane_row = lax.broadcasted_iota(jnp.int32, (16, BLOCK), 0)
+    zero = jnp.zeros((16, BLOCK), jnp.float32)
+    for r in range(SIDE):
+        a = jnp.broadcast_to(hi[r : r + 1, :].astype(jnp.float32), (16, BLOCK))
+        b = jnp.broadcast_to(mid[r : r + 1, :].astype(jnp.float32), (16, BLOCK))
+        c = jnp.broadcast_to(low[r : r + 1, :].astype(jnp.float32), (16, BLOCK))
+        both = jnp.where(lane_row == 0, a, jnp.where(lane_row == 1, b, jnp.where(lane_row == 2, c, zero)))
+        vp[r] = both.astype(jnp.bfloat16)
+    own_s = s_ref[pl.ds(own, 1), :]
+    own_lw = aux_ref[pl.ds(own, 1), :]
+    f_ref[...] = epsilon * own_lw - epsilon * (jnp.log(own_s) + ln2 * aux_ref[16:17, :]) + sq_ref[...]
+
+    acc[...] = jnp.zeros_like(acc)
+    count = count_ref[0]
+
+    def group(step, carry):
+        for u in range(UNROLL):
+            raw = step * UNROLL + u
+            slot = jnp.minimum(raw, count - 1)
+            part = lax.dot_general(
+                vp[row_ref[slot]], k_ref[slot], (((1,), (1,)), ((), ())),
+                preferred_element_type=jnp.float32,
+            )
+            acc[col_ref[slot]] += jnp.where(raw < count, part, 0.0)
+        return carry
+
+    lax.fori_loop(0, pl.cdiv(count, UNROLL), group, 0)
+    t_ref[...] = jnp.sum(acc[...], axis=1)
+
+
+def col_pass(count, row, col, own, total, aux, sq, kernel_tiles):
+    smem = pl.BlockSpec(memory_space=pltpu.SMEM)
+    vmem = pl.BlockSpec(memory_space=pltpu.VMEM)
+    return pl.pallas_call(
+        col_kernel,
+        out_shape=(
+            jax.ShapeDtypeStruct((1, BLOCK), jnp.float32),
+            jax.ShapeDtypeStruct((SIDE, BLOCK), jnp.float32),
+        ),
+        in_specs=[smem] * 4 + [vmem] * 4,
+        out_specs=[vmem] * 2,
+        scratch_shapes=[
+            pltpu.VMEM((SIDE, 16, BLOCK), jnp.bfloat16),
+            pltpu.VMEM((SIDE, 16, BLOCK), jnp.float32),
+        ],
+        compiler_params=pltpu.CompilerParams(vmem_limit_bytes=vmem_bytes),
+        name="col_pass",
+    )(count, row, col, own, total, aux, sq, kernel_tiles)
+
+
+def ring(k):
+    return [(i, (i // 4) * 4 + (i + k) % 4) for i in range(SIDE)]
+
+
+def hop(k):
+    return [(i, (i + 4 * k) % SIDE) for i in range(SIDE)]
+
+
+def swap(bit):
+    return [(i, i ^ bit) for i in range(SIDE)]
+
+
+def fast_form(x, y, lw, g, entries, count, tgt_id, src_id):
+    xp, yp, x_sq, y_sq = pack(x, y, lw, g)
+    xz = jnp.stack([xp] + [lax.ppermute(xp, "tgt", hop(k)) for k in (1, 2, 3)])
+    yh = jnp.stack([yp, lax.ppermute(yp, "src", swap(2))])
+    xs = [xz] + [lax.ppermute(xz, "tgt", ring(k)) for k in (1, 2, 3)]
+    yy = [yh] + [lax.ppermute(yh, "src", hop(k)) for k in (1, 2, 3)]
+    ys = [jnp.concatenate([a, lax.ppermute(a, "src", swap(1))]) for a in yy]
+
+    row = entries[:, 0] % SIDE
+    col = entries[:, 1] // SIDE
+    my_z, my_x = tgt_id // 4, tgt_id % 4
+    my_y, my_h, my_c = src_id // 4, (src_id // 2) % 2, src_id % 2
+    xat = ((my_x - row % 4) % 4) * 4 + (my_z - row // 4) % 4
+    yat = ((my_y - col // 4) % 4) * 4 + (my_c ^ (col % 2)) * 2 + (my_h ^ ((col // 2) % 2))
+    at = jnp.arange(SIDE, dtype=jnp.int32)
+    where = ((my_z - at % 4) % 4) * 4 + (my_x - at // 4) % 4
+
+    part, aux, tiles = row_pass(count, row, xat, yat, where, xs, ys)
+
+    def all_sum(a, shift):
+        far = [lax.ppermute(a, "tgt", shift(k)) for k in (1, 2, 3)]
+        return (a + far[1]) + (far[0] + far[2])
+
+    total = all_sum(all_sum(part, ring), hop)
+    f_own, t_part = col_pass(
+        count, row, col, tgt_id.reshape(1), total, aux, x_sq, tiles
+    )
+    t_all = lax.all_to_all(t_part, "src", 0, 0, tiled=True)
+    return f_own.reshape(BLOCK), jnp.sum(t_all, axis=0), ln2 * aux[18] * epsilon + y_sq.reshape(BLOCK)
+
+
+def on_device(
+    source_points, target_points, source_logw, target_logw, potential_in, pair_list, pair_counts
+):
+    tgt_id = lax.axis_index("tgt")
+    src_id = lax.axis_index("src")
+    f_own, t_own, offset = fast_form(
+        source_points, target_points, source_logw, potential_in, pair_list[0], pair_counts,
+        tgt_id, src_id,
+    )
+    g_own = epsilon * target_logw - epsilon * jnp.log(t_own) + offset
+    out_of_range = jnp.any(jnp.isnan(t_own))
+    return lax.cond(
+        out_of_range,
+        plain_form,
+        lambda *_: (f_own, g_own),
+        source_points, target_points, source_logw, target_logw, potential_in, pair_list, pair_counts,
+    )
 
 
 def solution(mesh):

time: 2400 us -> 2500 us (1.042)
  the two profiles are of different devices: /device:TPU:6 before, /device:TPU:2 now
where the time goes in v1:
time: 2500 us; the launch traced here: 2470 us
  blocking collectives  1340 us (54%)
  loops' own time  647 us (26%)
  matrix products  166 us (7%)
  local copies, waits for them, and re-layouts  119 us (5%)
  waiting for transfers between devices  104 us (4%)
  starting transfers between devices  43.8 us (2%)
    pmax x1, blocking collectives, plain_form(): col_high = lax.pmax(col_parts[0], 'src')  572 us
    pmax x1, blocking collectives, plain_form(): row_high = lax.pmax(row_parts[0], 'tgt')  546 us
    another operation x1, loops' own time, plain_form(): col_parts = lax.fori_loop(0, own_count, col_visit_pair, col_start)  328 us
    another operation x1, loops' own time, plain_form(): row_parts = lax.fori_loop(0, own_count, row_visit_pair, row_start)  319 us
    dot_general x126, matrix products, cross_cost(): lax.dot_general(left_points, right_points, (((0,), (0,)), ((), ())), prec...  166 us
    psum x1, blocking collectives, plain_form(): col_sum = lax.psum(col_parts[1] * jnp.exp(col_parts[0] - col_high), 'src')  84.1 us
    psum x1, blocking collectives, plain_form(): row_sum = lax.psum(row_parts[1] * jnp.exp(row_parts[0] - row_high), 'tgt')  76.4 us
    all_gather x1, waiting for transfers between devices, plain_form(): group_points = lax.all_gather(source_points, 'tgt', axis=1, tiled=True)  70.9 us
  transfers between devices with their start and end apart: 23, of which 14 were waited for; matrix products, arithmetic and copies ran while one was open for 0% of the time, Pallas kernels for 0%

profile of v1, /device:TPU:2, one launch (start us, length us, event | category | flops | bytes accessed | tf_op | source)
XLA Modules:
  0.0 2468.1 jit_solution(1074790626135673028)
XLA Ops:
  7.2 1.6 pack.1
  8.8 7.2 collective-permute-start.6
  16.0 1.9 collective-permute-start.2
  20.4 3.1 collective-permute-start.12
  25.7 1.4 collective-permute-done.1
  27.1 1.6 collective-permute-start.8
  31.0 2.1 collective-permute-start.4
  34.2 1.6 collective-permute-start.3
  37.2 2.3 collective-permute-done.5.x3
  39.5 7.2 collective-permute-done.4.x2
  47.6 8.0 row_pass.1
  55.6 1.7 collective-permute-start.16
  57.7 1.9 collective-permute-start.14
  59.6 1.4 collective-permute-done.15
  61.0 1.9 collective-permute-done.14
  63.0 8.8 collective-permute-start.19
  73.2 4.1 collective-permute-done.18
  78.0 5.3 col_pass.1
  84.0 9.1 all-to-all-start
  93.1 10.0 all-to-all-done
  104.4 2356.8 %conditional.1 = (f32[256]{0:T(256)}, f32[256]{0:T(256)}) conditional(s32[]{:T(128)} %convert_element_type.3, (f32[1,256]{1,0:T(1,128)}, f32[256]{0:T(256)S(1)}, f32[256]{0:T(256)S(1)}, f32[24,256]{1,0:T(8,128)S(1)}, f32[1,256]{1,0:T(1,128)S(1)}) %tuple.110, (f32[256]{0:T(256)S(1)}, s32[1]{0:T(128)}, s32[1,128,2]{1,2,0:T(2,128)S(1)}, ...), branch_computations={%region_2.3_spmd, %region_3.18_spmd} | conditional | flops 102804560 | bytes 10706772 | solution.py:377
  105.9 35.3 %all-gather = f32[16,1,256]{2,1,0:T(1,128)S(1)} all-gather(f32[1,1,256]{2,1,0:T(1,128)S(1)} %bitcast.78), channel_id=1, replica_groups=mesh['src'=16,'tgt'=16] {'tgt'}, dimensions={0}, use_global_device_ids=true | all-gather | bytes 17408 | tf_op jit(solution)/shard_map/cond/branch_1_fun/all_gather | solution.py:60
  141.3 25.1 %all-gather.1 = f32[16,1,256]{2,1,0:T(1,128)S(1)} all-gather(f32[1,1,256]{2,1,0:T(1,128)S(1)} %bitcast.80), channel_id=1, replica_groups=mesh['src'=16,'tgt'=16] {'src'}, dimensions={0}, use_global_device_ids=true | all-gather | bytes 17408 | tf_op jit(solution)/shard_map/cond/branch_1_fun/all_gather | solution.py:62
  166.4 1.3 multiply_reduce_fusion
  167.7 70.9 %all-gather.5.cloned.1.call-done = f32[64,4096]{1,0:T(8,128)} async-done(((f32[64,256]{1,0:T(8,128)}), f32[64,4096]{1,0:T(8,128)}) %all-gather.5.cloned.1.call-update) | async-done | bytes 1048592 | tf_op jit(solution)/shard_map/cond/branch_1_fun/all_gather | solution.py:59
  238.7 1.3 multiply_reduce_fusion.1
  240.0 465.9 %while.26 = (s32[]{:T(128)}, f32[16,256]{1,0:T(8,128)S(1)}, f32[16,256]{1,0:T(8,128)S(1)}, s32[]{:T(128)}, s32[128,2]{0,1:T(2,128)S(1)}, /*index=5*/f32[4096]{0:...) while((s32[]{:T(128)}, f32[16,256]{1,0:T(8,128)S(1)}, ...), condition=%wide.region_9.9_spmd, body=%wide.region_6.8_spmd.sunk | while | flops 50857000 | bytes 678540 | solution.py:88
  705.9 546.2 %pmax.12 = f32[16,256]{1,0:T(8,128)S(1)} all-reduce(f32[16,256]{1,0:T(8,128)S(1)} %get-tuple-element.313), channel_id=1, replica_groups=mesh['src'=16,'tgt'=16] {'tgt'}, use_global_device_ids=true, to_apply=%region_10.10 | all-reduce | flops 4096 | bytes 32768 | tf_op jit(solution)/shard_map/cond/branch_1_fun/pmax | solution.py:89
  1252.1 76.4 %psum.12 = f32[16,256]{1,0:T(8,128)S(1)} all-reduce(f32[16,256]{1,0:T(8,128)S(1)} %exponential_multiply_fusion.1), channel_id=1, replica_groups=mesh['src'=16,'tgt'=16] {'tgt'}, use_global_device_ids=true, to_apply=%region_11.11 | all-reduce | flops 4096 | bytes 32768 | tf_op jit(solution)/shard_map/cond/branch_1_fun/psum | solution.py:90
  1329.2 475.1 %while.27 = (s32[]{:T(128)}, f32[16,256]{1,0:T(8,128)S(1)}, f32[16,256]{1,0:T(8,128)S(1)}, s32[]{:T(128)}, s32[128,2]{0,1:T(2,128)S(1)}, /*index=5*/f32[4096]{0:...) while((s32[]{:T(128)}, f32[16,256]{1,0:T(8,128)S(1)}, ...), condition=%wide.region_15.15_spmd, body=%wide.region_12.14_spmd.sunk | while | flops 50857000 | bytes 678540 | solution.py:106
  1804.3 572.2 %pmax.13 = f32[16,256]{1,0:T(8,128)S(1)} all-reduce(f32[16,256]{1,0:T(8,128)S(1)} %get-tuple-element.316), channel_id=1, replica_groups=mesh['src'=16,'tgt'=16] {'src'}, use_global_device_ids=true, to_apply=%region_16.16 | all-reduce | flops 4096 | bytes 32768 | tf_op jit(solution)/shard_map/cond/branch_1_fun/pmax | solution.py:107
  2376.5 84.1 %psum.13 = f32[16,256]{1,0:T(8,128)S(1)} all-reduce(f32[16,256]{1,0:T(8,128)S(1)} %exponential_multiply_fusion), channel_id=1, replica_groups=mesh['src'=16,'tgt'=16] {'src'}, use_global_device_ids=true, to_apply=%region_17.17 | all-reduce | flops 4096 | bytes 32768 | tf_op jit(solution)/shard_map/cond/branch_1_fun/psum | solution.py:108
  (1200 shorter events, 310.6 us)
Async XLA Ops:
  7.2 97.2 %copy-start.2 = (f32[256]{0:T(256)S(1)}, f32[256]{0:T(256)}, u32[]{:S(2)}) copy-start(f32[256]{0:T(256)} %param.15) | copy-start | bytes 3076
  7.2 97.2 %copy-start.3 = (f32[256]{0:T(256)S(1)}, f32[256]{0:T(256)}, u32[]{:S(2)}) copy-start(f32[256]{0:T(256)} %param.17) | copy-start | bytes 3076
  7.2 97.2 %copy-start.1 = (s32[1,128,2]{1,2,0:T(2,128)S(1)}, s32[1,128,2]{1,2,0:T(2,128)}, u32[]{:S(2)}) copy-start(s32[1,128,2]{1,2,0:T(2,128)} %param.18) | copy-start | bytes 3076
  7.2 97.2 %copy-start.4 = (f32[256]{0:T(256)S(1)}, f32[256]{0:T(256)}, u32[]{:S(2)}) copy-start(f32[256]{0:T(256)} %param.16) | copy-start | bytes 3076
  8.8 10.7 collective-permute-start.6
  16.0 9.0 collective-permute-start.2
  18.0 9.1 collective-permute-start.1
  18.5 10.6 collective-permute-start
  20.4 8.6 collective-permute-start.12
  24.3 6.7 collective-permute-start.10
  25.0 8.2 collective-permute-start.7
  27.1 7.1 collective-permute-start.8
  29.1 6.8 collective-permute-start.13
  30.0 9.5 collective-permute-start.5
  31.0 15.7 collective-permute-start.4
  33.2 2.9 collective-permute-start.11
  34.2 13.4 collective-permute-start.3
  35.8 1.4 collective-permute-start.9
  55.6 4.0 collective-permute-start.16
  57.3 3.7 collective-permute-start.15
  57.7 5.2 collective-permute-start.14
  63.0 10.3 collective-permute-start.19
  71.8 5.5 collective-permute-start.18
  71.8 5.5 collective-permute-start.17
  77.3 0.7 copy-start
  84.0 19.1 all-to-all-start
  104.4 62.0 %all-gather.7.cloned.1.call-start = ((), (), s32[]{:S(2)}) async-start(), calls=%async_computation.2 | async-start | bytes 1114112 | tf_op jit(solution)/shard_map/cond/branch_1_fun/all_gather | solution.py:61
  105.2 133.5 %all-gather.5.cloned.1.call-start = ((), (), s32[]{:S(2)}) async-start(), calls=%async_computation.1 | async-start | bytes 1114112 | tf_op jit(solution)/shard_map/cond/branch_1_fun/all_gather | solution.py:59
Sparse Core Ops, SparseCore 0:
  107.8 52.4 all-gather.6
  162.2 76.4 all-gather.4

commit v2 on v0

--- a/solution.py
+++ b/solution.py
@@ -1,10 +1,23 @@
+import functools
+
 import jax
 import jax.numpy as jnp
 from jax import lax
+from jax.experimental import pallas as pl
+from jax.experimental.pallas import tpu as pltpu
 from jax.sharding import PartitionSpec as P
 
 epsilon = 0.25
 lowest_log = -1e30
+log2e = 1.4426950408889634
+ln2 = 0.6931471805599453
+SIDE = 16
+BLOCK = 256
+FEAT = 64
+ROWS = 72
+UNROLL = 8
+vmem_bytes = 24 * 1024 * 1024
+full_tiles = 128
 
 
 def merge_pair(first, second):
@@ -38,20 +51,22 @@
     )
 
 
-def on_device(
+def gather_blocks(points, axis):
+    copies = jnp.broadcast_to(points, (lax.axis_size(axis), *points.shape))
+    blocks = lax.all_to_all(copies, axis, 0, 0, tiled=True)
+    return jnp.moveaxis(blocks, 0, 1).reshape(points.shape[0], -1)
+
+
+def plain_form(
     source_points, target_points, source_logw, target_logw, potential_in, pair_list, pair_counts
 ):
     n_tgt = lax.axis_size("tgt")
     n_src = lax.axis_size("src")
     block_len = source_points.shape[1]
-    group_points, group_logw = (
-        lax.all_gather(source_points, "tgt", axis=1, tiled=True),
-        lax.all_gather(source_logw, "tgt", axis=0, tiled=True),
-    )
-    column_points, column_g = (
-        lax.all_gather(target_points, "src", axis=1, tiled=True),
-        lax.all_gather(potential_in, "src", axis=0, tiled=True),
-    )
+    group_points = gather_blocks(source_points, "tgt")
+    group_logw = lax.all_gather(source_logw, "tgt", axis=0, tiled=True)
+    column_points = gather_blocks(target_points, "src")
+    column_g = lax.all_gather(potential_in, "src", axis=0, tiled=True)
     group_sq = jnp.sum(group_points * group_points, axis=0)
     column_sq = jnp.sum(column_points * column_points, axis=0)
     row_start = (
@@ -102,6 +117,404 @@
     own_sum = lax.dynamic_slice_in_dim(col_sum, lax.axis_index("src"), 1, 0)[0]
     g_own = epsilon * target_logw - epsilon * (own_high + jnp.log(own_sum))
     return (f_own, g_own)
+
+
+smem = pl.BlockSpec(memory_space=pltpu.SMEM)
+vmem = pl.BlockSpec(memory_space=pltpu.VMEM)
+
+
+def f32(*shape):
+    return jax.ShapeDtypeStruct(shape, jnp.float32)
+
+
+def pack_kernel(
+    count_ref, ent_ref, x_ref, y_ref, lw_ref, g_ref, xp_ref, yp_ref, xsq_ref, ysq_ref, out_ref
+):
+    x = x_ref[...]
+    y = y_ref[...]
+    y_sq = jnp.sum(y * y, axis=0, keepdims=True)
+    b = (4.0 * log2e) * (g_ref[...] - y_sq)
+    row = lax.broadcasted_iota(jnp.int32, (8, BLOCK), 0)
+    b_max = jnp.max(b, axis=1, keepdims=True)
+    xp_ref[0:FEAT, :] = x
+    xp_ref[FEAT:ROWS, :] = jnp.where(row == 0, lw_ref[...], b_max)
+    yp_ref[0:FEAT, :] = y
+    yp_ref[FEAT:ROWS, :] = jnp.broadcast_to(b, (8, BLOCK))
+    xsq_ref[...] = jnp.sum(x * x, axis=0, keepdims=True)
+    ysq_ref[...] = y_sq
+    tgt_id, src_id, count = lax.axis_index("tgt"), lax.axis_index("src"), count_ref[0]
+    my_z, my_x = tgt_id // 4, tgt_id % 4
+    my_y, my_h, my_c = src_id // 4, (src_id // 2) % 2, src_id % 2
+    lane = lax.broadcasted_iota(jnp.int32, (1, full_tiles), 1)
+    live = lane < count
+
+    def ordered(key, code):
+        tall = jnp.broadcast_to(key, (full_tiles, full_tiles)).T
+        rank = jnp.sum(jnp.where(tall < key, 1, 0), axis=0, keepdims=True)
+        spot = jnp.broadcast_to(rank, (full_tiles, full_tiles)).T
+        tall_code = jnp.broadcast_to(code, (full_tiles, full_tiles)).T
+        return jnp.sum(jnp.where(spot == lane, tall_code, 0), axis=0, keepdims=True)
+
+    def how_many(mask):
+        return jnp.sum(jnp.where(mask, 1, 0), axis=1, keepdims=True)
+
+    row = ent_ref[0:1, :] & 15
+    col = ent_ref[1:2, :] >> 4
+    q = (my_x - (row & 3)) & 3
+    p = (my_z - (row >> 2)) & 3
+    h = ((col >> 1) & 1) ^ my_h
+    c = (col & 1) ^ my_c
+    yat = ((my_y - (col >> 2)) & 3) * 4 + c * 2 + h
+    dy = (col >> 2) ^ my_y
+    spot = h * 8 + c * 4 + (dy ^ (dy >> 1))
+    stage = jnp.where(q == 0, 0, jnp.where(q == 2, 2, 1))
+    code = row + spot * 16 + (q * 4 + p) * 256 + yat * 4096
+    code = ordered(jnp.where(live, stage, 3) * 128 + lane, jnp.where(live, code, 0))
+    far = (code & 128) != 0
+    code_b = (code & 127) + lane * 256
+    code_b = ordered(jnp.where(live, jnp.where(far, 0, 1), 2) * 128 + lane, code_b)
+    out_ref[0:1, :] = code
+    out_ref[1:2, :] = code_b
+    first = how_many(live & (stage == 0))
+    second = how_many(live & (stage <= 1))
+    away = how_many(live & far)
+    out_ref[2:3, :] = jnp.where(lane == 0, first, jnp.where(lane == 1, second, jnp.where(lane == 2, away, count)))
+    out_ref[3:8, :] = jnp.zeros((5, full_tiles), jnp.int32)
+
+
+def pack(count, entries, x, y, lw, g):
+    return pl.pallas_call(
+        pack_kernel,
+        out_shape=(
+            f32(ROWS, BLOCK), f32(ROWS, BLOCK), f32(1, BLOCK), f32(1, BLOCK),
+            jax.ShapeDtypeStruct((8, full_tiles), jnp.int32),
+        ),
+        in_specs=[smem] + [vmem] * 5,
+        out_specs=[vmem] * 5,
+        name="pack",
+    )(count, entries.T, x, y, lw.reshape(1, BLOCK), g.reshape(1, BLOCK))
+
+
+def prepare_source(x, at, xa):
+    x = x * (8.0 * log2e)
+    hi = x.astype(jnp.bfloat16)
+    lo = (x - hi.astype(jnp.float32)).astype(jnp.bfloat16)
+    xa[at, 0:64, :] = hi
+    xa[at, 64:128, :] = lo
+    xa[at, 128:192, :] = hi
+    xa[at, 192:256, :] = lo
+
+
+def note_source(block, q, p, aux_ref):
+    tgt_id = lax.axis_index("tgt")
+    where = ((tgt_id // 4 - p) & 3) * 4 + ((tgt_id % 4 - q) & 3)
+    mean = jnp.sum(block[0:FEAT], axis=1, keepdims=True) * (1.0 / BLOCK)
+    aux_ref[pl.ds(where, 1), :] = block[FEAT : FEAT + 1]
+    aux_ref[16:17, :] = jnp.maximum(aux_ref[16:17, :], block[FEAT + 1 : FEAT + 2])
+    aux_ref[17:18, :] = jnp.maximum(aux_ref[17:18, :], jnp.sum(mean * mean, axis=0, keepdims=True))
+
+
+def visit_tiles(plan_ref, begin, end, slot_of, xa, ya, ub, k_ref, acc_ref):
+    def group(step, carry):
+        for u in range(UNROLL):
+            raw = begin + step * UNROLL + u
+            slot = jnp.minimum(raw, end - 1)
+            code = plan_ref[0, slot]
+            xat = slot_of((code >> 8) & 15)
+            yat = (code >> 12) & 15
+            row = code & 15
+            scores = jnp.dot(ya[yat], xa[xat], preferred_element_type=jnp.float32)
+            tile = jnp.exp2(scores)
+            k_ref[slot] = tile.astype(jnp.bfloat16)
+            weight = ub[yat]
+            left = jnp.sum((tile[:, 0:128] * weight).reshape(32, 8, 128), axis=0)
+            right = jnp.sum((tile[:, 128:256] * weight).reshape(32, 8, 128), axis=0)
+            live = raw < end
+            acc_ref[row, :, 0:128] += jnp.where(live, left, 0.0)
+            acc_ref[row, :, 128:256] += jnp.where(live, right, 0.0)
+        return carry
+
+    lax.fori_loop(0, pl.cdiv(end - begin, UNROLL), group, 0)
+
+
+def first_kernel(
+    plan_ref, x0, y0, z0, y1, z1, y2, z2, y3, z3,
+    ya, ub, k_ref, acc_ref, aux_ref, stat_ref, xa, codes, sem,
+):
+    fetch = pltpu.make_async_copy(plan_ref, codes, sem)
+    fetch.start()
+    ys = (y0, z0, y1, z1, y2, z2, y3, z3)
+    lines = [ys[at // 2][at % 2, FEAT : FEAT + 1, :] for at in range(SIDE)]
+    top = jnp.max(functools.reduce(jnp.maximum, lines), axis=1, keepdims=True)
+    low = jnp.min(functools.reduce(jnp.minimum, lines), axis=1, keepdims=True) - top
+    y_sq = jnp.zeros((1, BLOCK), jnp.float32)
+    for at in range(SIDE):
+        y = ys[at // 2][at % 2, 0:FEAT, :]
+        y_sq = jnp.maximum(y_sq, jnp.sum(y * y, axis=0, keepdims=True))
+        turned = jnp.concatenate([y, y], axis=0).T
+        hi = turned.astype(jnp.bfloat16)
+        lo = (turned - hi.astype(jnp.float32)).astype(jnp.bfloat16)
+        ya[at, :, 0:128] = hi
+        ya[at, :, 128:256] = lo
+        ub[at] = jnp.exp2(jnp.broadcast_to(lines[at] - top, (128, BLOCK)).T)
+    stat_ref[0:1, :] = jnp.broadcast_to(low, (1, BLOCK))
+    stat_ref[1:2, :] = jnp.broadcast_to(top, (1, BLOCK))
+    stat_ref[2:3, :] = y_sq
+    stat_ref[3:8, :] = jnp.zeros((5, BLOCK), jnp.float32)
+    aux_ref[0:16, :] = jnp.zeros((16, BLOCK), jnp.float32)
+    aux_ref[16:17, :] = jnp.full((1, BLOCK), -1e30, jnp.float32)
+    aux_ref[17:24, :] = jnp.zeros((7, BLOCK), jnp.float32)
+    for p in range(4):
+        block = x0[p]
+        prepare_source(block[0:FEAT], p, xa)
+        note_source(block, 0, p, aux_ref)
+    acc_ref[...] = jnp.zeros_like(acc_ref)
+    fetch.wait()
+    visit_tiles(codes, 0, codes[2, 0], lambda at: at, xa, ya, ub, k_ref, acc_ref)
+
+
+def second_kernel(
+    plan_ref, x1, x3, ya, ub, k_in, acc_in, aux_in, k_ref, acc_ref, aux_ref, xa, codes, sem
+):
+    fetch = pltpu.make_async_copy(plan_ref, codes, sem)
+    fetch.start()
+    aux_ref[...] = aux_in[...]
+    acc_ref[...] = acc_in[...]
+    for q, x_ref, base in ((1, x1, 0), (3, x3, 4)):
+        for p in range(4):
+            block = x_ref[p]
+            prepare_source(block[0:FEAT], base + p, xa)
+            note_source(block, q, p, aux_ref)
+    fetch.wait()
+    visit_tiles(
+        codes, codes[2, 0], codes[2, 1],
+        lambda at: (at & 3) + ((at >> 3) & 1) * 4, xa, ya, ub, k_ref, acc_ref,
+    )
+
+
+def third_kernel(
+    plan_ref, xl, xr, ya, ub, k_in, acc_in, aux_in, stat_ref, k_ref, s_ref, aux_ref, xa, acc, codes, sem
+):
+    fetch = pltpu.make_async_copy(plan_ref, codes, sem)
+    fetch.start()
+    aux_ref[...] = aux_in[...]
+    acc[...] = acc_in[...]
+    for p in range(4):
+        block = xl[p] if p < 2 else xr[p - 2]
+        prepare_source(block[0:FEAT], p, xa)
+        note_source(block, 2, p, aux_ref)
+    fetch.wait()
+    visit_tiles(codes, codes[2, 1], codes[2, 3], lambda at: at & 3, xa, ya, ub, k_ref, acc)
+    total = jnp.sum(acc[...], axis=1)
+    low = stat_ref[0:1, 0:1]
+    top = stat_ref[1:2, 0:1]
+    shift = aux_ref[16:17, 0:1]
+    lean = (8.0 * log2e) * jnp.sqrt(aux_ref[17:18, 0:1] * jnp.max(stat_ref[2:3, :], axis=1, keepdims=True))
+    most = jnp.max(jnp.max(total, axis=0, keepdims=True), axis=1, keepdims=True)
+    apart = top - shift
+    good = (
+        (lean <= 24.0)
+        & (low >= -105.0)
+        & (jnp.abs(apart) <= 16.0)
+        & (most <= jnp.exp2(120.0 + low))
+    )
+    s_ref[...] = jnp.where(good, total * jnp.exp2(apart), jnp.nan)
+    aux_ref[18:19, :] = jnp.broadcast_to(apart, (1, BLOCK))
+
+
+tiles_shape = pltpu.VMEM((full_tiles, BLOCK, BLOCK), jnp.bfloat16)
+target_shape = pltpu.VMEM((SIDE, BLOCK, BLOCK), jnp.bfloat16)
+weight_shape = pltpu.VMEM((SIDE, BLOCK, 128), jnp.float32)
+row_cost = dict(flops=32 * 2 * BLOCK**3, bytes_accessed=1 << 20, transcendentals=32 * BLOCK * BLOCK)
+
+
+codes_scratch = [pltpu.SMEM((8, full_tiles), jnp.int32), pltpu.SemaphoreType.DMA]
+
+
+def source_scratch(blocks):
+    return pltpu.VMEM((blocks, BLOCK, BLOCK), jnp.bfloat16)
+
+
+def first_pass(order, x0, ys):
+    return pl.pallas_call(
+        first_kernel,
+        out_shape=(
+            target_shape, weight_shape, tiles_shape,
+            f32(SIDE, 8, BLOCK), f32(24, BLOCK), f32(8, BLOCK),
+        ),
+        in_specs=[vmem] * 10,
+        out_specs=[vmem] * 6,
+        scratch_shapes=[source_scratch(4), *codes_scratch],
+        compiler_params=pltpu.CompilerParams(vmem_limit_bytes=vmem_bytes),
+        cost_estimate=pl.CostEstimate(**row_cost),
+        name="row_pass_a",
+    )(order, x0, *ys)
+
+
+def second_pass(order, x1, x3, ya, ub, tiles, acc, aux):
+    return pl.pallas_call(
+        second_kernel,
+        out_shape=(tiles_shape, f32(SIDE, 8, BLOCK), f32(24, BLOCK)),
+        in_specs=[vmem] * 8,
+        out_specs=[vmem] * 3,
+        scratch_shapes=[source_scratch(8), *codes_scratch],
+        input_output_aliases={5: 0},
+        compiler_params=pltpu.CompilerParams(vmem_limit_bytes=vmem_bytes),
+        cost_estimate=pl.CostEstimate(**row_cost),
+        name="row_pass_b",
+    )(order, x1, x3, ya, ub, tiles, acc, aux)
+
+
+def third_pass(order, xl, xr, ya, ub, tiles, acc, aux, stat):
+    return pl.pallas_call(
+        third_kernel,
+        out_shape=(tiles_shape, f32(SIDE, BLOCK), f32(24, BLOCK)),
+        in_specs=[vmem] * 9,
+        out_specs=[vmem] * 3,
+        scratch_shapes=[source_scratch(4), pltpu.VMEM((SIDE, 8, BLOCK), jnp.float32), *codes_scratch],
+        input_output_aliases={5: 0},
+        compiler_params=pltpu.CompilerParams(vmem_limit_bytes=vmem_bytes),
+        cost_estimate=pl.CostEstimate(**row_cost),
+        name="row_pass_c",
+    )(order, xl, xr, ya, ub, tiles, acc, aux, stat)
+
+
+def visit_columns(plan_ref, begin, end, v_ref, k_ref, t_ref, acc):
+    acc[...] = jnp.zeros_like(acc)
+
+    def group(step, carry):
+        for u in range(UNROLL):
+            raw = begin + step * UNROLL + u
+            code = plan_ref[1, jnp.minimum(raw, end - 1)]
+            v = jnp.where(raw < end, v_ref[pl.ds(code & 15, 1), :], 0.0)
+            tile = k_ref[code >> 8].astype(jnp.float32)
+            acc[(code >> 4) & 7] += tile[:, 0:128] * v[:, 0:128] + tile[:, 128:256] * v[:, 128:256]
+        return carry
+
+    lax.fori_loop(0, pl.cdiv(end - begin, UNROLL), group, 0)
+    ones = jnp.ones((16, 128), jnp.bfloat16)
+    across = (((1,), (1,)), ((), ()))
+    for c in range(8):
+        rest = acc[c]
+        total = jnp.zeros((16, BLOCK), jnp.float32)
+        for _ in range(3):
+            part = rest.astype(jnp.bfloat16)
+            rest = rest - part.astype(jnp.float32)
+            total += lax.dot_general(ones, part, across, preferred_element_type=jnp.float32)
+        t_ref[c : c + 1, :] = total[0:1, :]
+
+
+def far_kernel(plan_ref, s_ref, aux_ref, xsq_ref, k_ref, f_ref, v_ref, t_ref, acc, codes, sem):
+    fetch = pltpu.make_async_copy(plan_ref, codes, sem)
+    fetch.start()
+    total = s_ref[...]
+    v = jnp.exp(aux_ref[0:16, :]) / total * jnp.exp2(aux_ref[18:19, :])
+    fine = jnp.where((total >= 1.5e-11) & (total <= 4.3e12), 1.0, 0.0)
+    fine = jnp.min(jnp.min(fine, axis=1, keepdims=True), axis=0, keepdims=True) > 0.5
+    v_ref[...] = jnp.where(fine, v, jnp.nan)
+    own = lax.axis_index("tgt")
+    own_s = s_ref[pl.ds(own, 1), :]
+    own_lw = aux_ref[pl.ds(own, 1), :]
+    f_ref[...] = epsilon * own_lw - epsilon * (jnp.log(own_s) + ln2 * aux_ref[16:17, :]) + xsq_ref[...]
+    fetch.wait()
+    visit_columns(codes, 0, codes[2, 2], v_ref, k_ref, t_ref, acc)
+    t_ref[...] += jnp.where(fine, 0.0, jnp.nan)
+
+
+def near_kernel(plan_ref, v_ref, k_ref, t_ref, acc, codes, sem):
+    fetch = pltpu.make_async_copy(plan_ref, codes, sem)
+    fetch.start()
+    fetch.wait()
+    visit_columns(codes, codes[2, 2], codes[2, 3], v_ref, k_ref, t_ref, acc)
+
+
+def far_pass(order, total, aux, xsq, tiles):
+    return pl.pallas_call(
+        far_kernel,
+        out_shape=(f32(1, BLOCK), f32(SIDE, BLOCK), f32(8, BLOCK)),
+        in_specs=[vmem] * 5,
+        out_specs=[vmem] * 3,
+        scratch_shapes=[pltpu.VMEM((8, BLOCK, 128), jnp.float32), *codes_scratch],
+        compiler_params=pltpu.CompilerParams(vmem_limit_bytes=vmem_bytes),
+        cost_estimate=pl.CostEstimate(**row_cost),
+        name="col_pass_a",
+    )(order, total, aux, xsq, tiles)
+
+
+def near_pass(order, v, tiles):
+    return pl.pallas_call(
+        near_kernel,
+        out_shape=f32(8, BLOCK),
+        in_specs=[vmem] * 3,
+        out_specs=vmem,
+        scratch_shapes=[pltpu.VMEM((8, BLOCK, 128), jnp.float32), *codes_scratch],
+        compiler_params=pltpu.CompilerParams(vmem_limit_bytes=vmem_bytes),
+        cost_estimate=pl.CostEstimate(**row_cost),
+        name="col_pass_b",
+    )(order, v, tiles)
+
+
+def ring(k):
+    return [(i, (i // 4) * 4 + (i + k) % 4) for i in range(SIDE)]
+
+
+def hop(k):
+    return [(i, (i + 4 * k) % SIDE) for i in range(SIDE)]
+
+
+def swap(bits):
+    return [(i, i ^ bits) for i in range(SIDE)]
+
+
+def fast_form(x, y, lw, g, entries, count):
+    xp, yp, x_sq, y_sq, order = pack(count, entries, x, y, lw, g)
+    xz = jnp.stack([xp] + [lax.ppermute(xp, "tgt", hop(k)) for k in (1, 2, 3)])
+    yh = jnp.stack([yp, lax.ppermute(yp, "src", swap(2))])
+    x1 = lax.ppermute(xz, "tgt", ring(1))
+    x3 = lax.ppermute(xz, "tgt", ring(3))
+    yy = [yh] + [lax.ppermute(yh, "src", hop(k)) for k in (1, 2, 3)]
+    xl = lax.ppermute(x1[0:2], "tgt", ring(1))
+    xr = lax.ppermute(x3[2:4], "tgt", ring(3))
+    ys = [z for a in yy for z in (a, lax.ppermute(a, "src", swap(1)))]
+
+    ya, ub, tiles, acc, aux, stat = first_pass(order, xz, ys)
+    tiles, acc, aux = second_pass(order, x1, x3, ya, ub, tiles, acc, aux)
+    tiles, total, aux = third_pass(order, xl, xr, ya, ub, tiles, acc, aux, stat)
+
+    def all_sum(a, shift):
+        far = [lax.ppermute(a, "tgt", shift(k)) for k in (1, 2, 3)]
+        return (a + far[1]) + (far[0] + far[2])
+
+    total = all_sum(all_sum(total, ring), hop)
+
+    f_own, v, away = far_pass(order, total, aux, x_sq, tiles)
+    from_far = lax.ppermute(away, "src", swap(2))
+    part = near_pass(order, v, tiles) + from_far
+    part = part[0:4] + lax.ppermute(part[4:8], "src", swap(1))
+    part = (
+        part[0:1]
+        + lax.ppermute(part[1:2], "src", swap(4))
+        + lax.ppermute(part[2:3], "src", swap(12))
+        + lax.ppermute(part[3:4], "src", swap(8))
+    )
+    offset = epsilon * ln2 * stat[1] + y_sq.reshape(BLOCK)
+    return f_own.reshape(BLOCK), part.reshape(BLOCK), offset
+
+
+def on_device(
+    source_points, target_points, source_logw, target_logw, potential_in, pair_list, pair_counts
+):
+    f_own, t_own, offset = fast_form(
+        source_points, target_points, source_logw, potential_in, pair_list[0], pair_counts
+    )
+    g_own = epsilon * target_logw - epsilon * jnp.log(t_own) + offset
+    out_of_range = jnp.isnan(t_own[0])
+    return lax.cond(
+        out_of_range,
+        plain_form,
+        lambda *_: (f_own, g_own),
+        source_points, target_points, source_logw, target_logw, potential_in, pair_list, pair_counts,
+    )
 
 
 def solution(mesh):

time: 2400 us -> 2460 us (1.025)
  the two profiles are of different devices: /device:TPU:6 before, /device:TPU:0 now
where the time goes in v2:
time: 2460 us; the launch traced here: 2420 us
  loops' own time  1040 us (42%)
  blocking collectives  816 us (33%)
  matrix products  262 us (11%)
  local copies, waits for them, and re-layouts  202 us (8%)
  starting transfers between devices  48.7 us (2%)
    another operation x1, loops' own time, plain_form(): row_parts = lax.fori_loop(0, own_count, row_visit_pair, row_start)  518 us
    another operation x1, loops' own time, plain_form(): col_parts = lax.fori_loop(0, own_count, col_visit_pair, col_start)  518 us
    pmax x1, blocking collectives, plain_form(): col_high = lax.pmax(col_parts[0], 'src')  398 us
    dot_general x204, matrix products, cross_cost(): lax.dot_general(left_points, right_points, (((0,), (0,)), ((), ())), prec...  262 us
    pmax x1, blocking collectives, plain_form(): row_high = lax.pmax(row_parts[0], 'tgt')  146 us
    psum x1, blocking collectives, plain_form(): col_sum = lax.psum(col_parts[1] * jnp.exp(col_parts[0] - col_high), 'src')  84.1 us
    psum x1, blocking collectives, plain_form(): row_sum = lax.psum(row_parts[1] * jnp.exp(row_parts[0] - row_high), 'tgt')  74.2 us
    dynamic_slice x102, local copies, waits for them, and re-layouts, row_visit_pair(): row_id = own_entries[slot_id, 0] % n_tgt  66.9 us
  transfers between devices with their start and end apart: 27, of which 9 were waited for; matrix products, arithmetic and copies ran while one was open for 0% of the time, Pallas kernels for 0%

profile of v2, /device:TPU:0, one launch (start us, length us, event | category | flops | bytes accessed | tf_op | source)
XLA Modules:
  0.0 2422.4 jit_solution(6177131120201967699)
XLA Ops:
  1.3 2.0 pack.1
  3.5 3.3 collective-permute-start.1
  7.7 5.4 collective-permute-start.7
  18.0 1.6 collective-permute-start.9
  19.7 2.8 collective-permute-start.5
  22.4 2.9 collective-permute-start.11
  26.7 2.4 collective-permute-done.11.y2
  31.3 3.3 collective-permute-start.6
  35.3 3.4 row_pass_a.1
  38.7 4.2 row_pass_b.1
  42.9 2.8 row_pass_c.1
  45.9 3.2 collective-permute-start.17
  49.1 1.9 collective-permute-done.15
  51.0 3.3 collective-permute-start.18
  54.8 3.4 collective-permute-start.20
  58.2 1.7 collective-permute-done.19
  60.0 3.0 col_pass_a.1
  63.0 4.3 collective-permute-start.21
  67.3 2.9 col_pass_b.1
  73.9 2.1 collective-permute-start.25
  77.1 1.9 collective-permute-done.25
  80.9 2341.5 %conditional.1 = (f32[256]{0:T(256)}, f32[256]{0:T(256)}) conditional(s32[]{:T(128)} %bitcast.30, (f32[1,256]{1,0:T(1,128)}, f32[256]{0:T(256)S(1)}, f32[1,256]{1,0:T(1,128)S(1)}, f32[8,256]{1,0:T(8,128)S(1)}, f32[1,256]{1,0:T(1,128)S(1)}) %tuple.111, (f32[256]{0:T(256)S(1)}, s32[1]{0:T(128)}, s32[1,128,2]{1,2,0:T(2,128)S(1)}, ...), branch_computations={%region_0.0_spmd, %region_1.16_spmd} | conditional | flops 102804560 | bytes 15752980 | solution.py:512
  81.0 33.1 %all_to_all.8 = f32[16,64,256]{2,1,0:T(8,128)S(1)} all-to-all(f32[16,64,256]{2,1,0:T(8,128)S(1)} %broadcast_in_dim.0), channel_id=1, replica_groups=mesh['src'=16,'tgt'=16] {'tgt'}, dimensions={0} | all-to-all | bytes 2097152 | tf_op jit(solution)/shard_map/cond/branch_1_fun/all_to_all | solution.py:56
  115.2 5.7 all-to-all-start.1
  120.9 36.2 %all-gather.1 = f32[16,1,256]{2,1,0:T(1,128)S(1)} all-gather(f32[1,1,256]{2,1,0:T(1,128)S(1)} %bitcast.91), channel_id=1, replica_groups=mesh['src'=16,'tgt'=16] {'src'}, dimensions={0}, use_global_device_ids=true | all-gather | bytes 17408 | tf_op jit(solution)/shard_map/cond/branch_1_fun/all_gather | solution.py:69
  157.1 45.0 %all-gather = f32[16,1,256]{2,1,0:T(1,128)S(1)} all-gather(f32[1,1,256]{2,1,0:T(1,128)S(1)} %bitcast.89), channel_id=1, replica_groups=mesh['src'=16,'tgt'=16] {'tgt'}, dimensions={0}, use_global_device_ids=true | all-gather | bytes 17408 | tf_op jit(solution)/shard_map/cond/branch_1_fun/all_gather | solution.py:67
  203.6 758.4 %while.26 = (s32[]{:T(128)}, f32[16,256]{1,0:T(8,128)S(1)}, f32[16,256]{1,0:T(8,128)S(1)}, s32[]{:T(128)}, s32[128,2]{0,1:T(2,128)S(1)}, /*index=5*/f32[4096]{0:...) while((s32[]{:T(128)}, f32[16,256]{1,0:T(8,128)S(1)}, ...), condition=%wide.region_7.7_spmd, body=%wide.region_4.6_spmd.sunk | while | flops 50857000 | bytes 678532 | solution.py:95
  962.1 145.6 %pmax.12 = f32[16,256]{1,0:T(8,128)S(1)} all-reduce(f32[16,256]{1,0:T(8,128)S(1)} %get-tuple-element.314), channel_id=1, replica_groups=mesh['src'=16,'tgt'=16] {'tgt'}, use_global_device_ids=true, to_apply=%region_8.8 | all-reduce | flops 4096 | bytes 32768 | tf_op jit(solution)/shard_map/cond/branch_1_fun/pmax | solution.py:96
  1107.7 74.2 %psum.12 = f32[16,256]{1,0:T(8,128)S(1)} all-reduce(f32[16,256]{1,0:T(8,128)S(1)} %exponential_multiply_fusion.1), channel_id=1, replica_groups=mesh['src'=16,'tgt'=16] {'tgt'}, use_global_device_ids=true, to_apply=%region_9.9 | all-reduce | flops 4096 | bytes 32768 | tf_op jit(solution)/shard_map/cond/branch_1_fun/psum | solution.py:97
  1182.0 757.4 %while.27 = (s32[]{:T(128)}, f32[16,256]{1,0:T(8,128)S(1)}, f32[16,256]{1,0:T(8,128)S(1)}, s32[]{:T(128)}, s32[128,2]{0,1:T(2,128)S(1)}, /*index=5*/f32[4096]{0:...) while((s32[]{:T(128)}, f32[16,256]{1,0:T(8,128)S(1)}, ...), condition=%wide.region_13.13_spmd, body=%wide.region_10.12_spmd.sunk | while | flops 50857000 | bytes 678532 | solution.py:113
  1939.4 397.6 %pmax.13 = f32[16,256]{1,0:T(8,128)S(1)} all-reduce(f32[16,256]{1,0:T(8,128)S(1)} %get-tuple-element.317), channel_id=1, replica_groups=mesh['src'=16,'tgt'=16] {'src'}, use_global_device_ids=true, to_apply=%region_14.14 | all-reduce | flops 4096 | bytes 32768 | tf_op jit(solution)/shard_map/cond/branch_1_fun/pmax | solution.py:114
  2337.0 84.1 %psum.13 = f32[16,256]{1,0:T(8,128)S(1)} all-reduce(f32[16,256]{1,0:T(8,128)S(1)} %exponential_multiply_fusion), channel_id=1, replica_groups=mesh['src'=16,'tgt'=16] {'src'}, use_global_device_ids=true, to_apply=%region_15.15 | all-reduce | flops 4096 | bytes 32768 | tf_op jit(solution)/shard_map/cond/branch_1_fun/psum | solution.py:115
  (1925 shorter events, 499.7 us)
Async XLA Ops:
  3.3 9.9 collective-permute-start
  3.5 9.7 collective-permute-start.1
  6.7 6.4 collective-permute-start.2
  7.7 9.4 collective-permute-start.7
  14.1 16.6 collective-permute-start.3
  18.0 8.7 collective-permute-start.9
  19.7 11.5 collective-permute-start.5
  22.4 6.6 collective-permute-start.11
  25.3 5.3 collective-permute-start.13
  26.7 4.6 collective-permute-start.8
  29.1 5.5 collective-permute-start.10
  30.6 4.0 collective-permute-start.12
  30.6 4.0 collective-permute-start.14
  31.2 11.7 collective-permute-start.4
  31.3 11.6 collective-permute-start.6
  38.7 21.3 copy-start.1
  38.7 21.3 copy-start.2
  45.7 5.3 collective-permute-start.15
  45.8 5.2 collective-permute-start.16
  45.9 5.2 collective-permute-start.17
  51.0 7.2 collective-permute-start.18
  54.4 5.5 collective-permute-start.19
  54.8 5.1 collective-permute-start.20
  60.0 20.8 copy-start.3
  60.0 20.8 copy-start.4
  60.0 20.8 copy-start.5
  63.0 7.6 collective-permute-start.21
  70.7 1.2 collective-permute-start.22
  71.9 4.2 collective-permute-start.23
  72.3 4.8 collective-permute-start.24
  73.9 5.1 collective-permute-start.25
  115.2 87.1 %all-to-all-start.1 = ((f32[16,64,256]{2,1,0:T(8,128)}), f32[16,64,256]{2,1,0:T(8,128)S(1)}, u32[]{:S(2)}, u32[]{:S(2)}) async-start(f32[16,64,256]{2,1,0:T(8,128)} %broadcast_in_dim.1), calls=%async_computation.1 | async-start | bytes 2097152 | tf_op jit(solution)/shard_map/cond/branch_1_fun/all_to_all | solution.py:56
  (4 other events, 63.2 us)
